TPU v7x, 512 devices: a whole 4x4x16 slice. The times are simulated.
512 devices in a mesh: segment: 32 (over z, core), neuron: 16 (over y, x).
Axes of the slice: x: 4, y: 4, z: 16, core: 2. Of those that a mesh axis runs over, the one named last changes fastest.
Arguments:
- pending_minibatch: bfloat16 [32, 8, 65536], P('segment', None, 'neuron'), may hold values from 0 to 32
- arriving_minibatches: bfloat16 [1, 8, 65536], P(None, None, 'neuron'), may hold values from 0 to 32
- coefficient_tiles: bfloat16 [32, 2, 4, 64, 65536], P('segment', None, None, None, 'neuron'), may hold values from -0.375 to 0.375
- offset_vector: float32 [32, 2, 65536], P('segment', None, 'neuron'), may hold values from -4 to 2
- source_tile_lookup: int32 [32, 2, 4, 1024], P('segment', None, None, 'neuron'), may hold values from 0 to 1023, as said below
- depth_of_segment: int32 [32], P('segment'), may hold values from 1 to 2, as said below
Outputs:
- section_out: bfloat16 [32, 8, 65536], P('segment', None, 'neuron')
Inputs may be any that keep to these rules, and one draw needn't show every extreme that they name: `depth_of_segment`: every section has at least one layer and some section has 2. `source_tile_lookup`: for each section, layer and group of 64 consecutive output blocks, the 256 entries name input blocks from each of the 16 groups of 64 consecutive input blocks exactly equally often.
All inputs are finite; a program needn't handle non-finite values.
Results may differ from a plain program's by a relative error of at most 0.0051.
Values may be sent and summed in bfloat16 or wider, within the bound.
A program may use at most 128 MiB of HBM per device.

v0:
```python
import jax
import jax.numpy as jnp
from jax import lax
from jax.sharding import PartitionSpec as P

BLK = 64
KB = 4
LMAX = 2


def shifted(value, axis, by):
    size = lax.axis_size(axis)
    pairs = [(i, i + by) for i in range(size) if 0 <= i + by < size]
    return lax.ppermute(value, axis, pairs)


def run_layer(y, w, b, idx):
    rows = y.shape[0]
    blocks_here = idx.shape[1]
    w_blocks = w.reshape(KB, BLK, blocks_here, BLK)
    cols = idx[:, :, None] * BLK + jnp.arange(BLK, dtype=jnp.int32)[None, None, :]
    full = lax.all_gather(y, "neuron", axis=1, tiled=True)
    taken = jnp.take(full, cols.reshape(-1), axis=1).reshape(rows, KB, blocks_here, BLK)
    acc = jnp.einsum("bkjr,krjc->bjc", taken, w_blocks, preferred_element_type=jnp.float32)
    acc = acc.reshape(rows, blocks_here * BLK)
    return jnp.clip(acc + b[None, :], 0.0, 32.0).astype(jnp.bfloat16)


def apply_layer_section(y, coefficient_tiles, offset_vector, source_tile_lookup, stored_tile_total):
    for level in range(LMAX):
        fresh = run_layer(
            y, coefficient_tiles[level], offset_vector[level], source_tile_lookup[level]
        )
        y = jnp.where(level < stored_tile_total, fresh, y)
    return y


def per_device(
    pending_minibatch,
    arriving_minibatches,
    coefficient_tiles,
    offset_vector,
    source_tile_lookup,
    depth_of_segment,
):
    coefficient_slice_local = coefficient_tiles[0]
    offset_slice_local = offset_vector[0]
    slice_tile_lookup = source_tile_lookup[0]
    stored_tile_total = depth_of_segment[0]
    activation_matrix = apply_layer_section(
        pending_minibatch[0],
        coefficient_slice_local,
        offset_slice_local,
        slice_tile_lookup,
        stored_tile_total,
    )
    first_phase = lax.axis_index("segment") == 0
    moved = shifted(activation_matrix, "segment", 1)
    moved = jnp.where(first_phase, arriving_minibatches[0], moved)
    activation_matrix = apply_layer_section(
        moved, coefficient_slice_local, offset_slice_local, slice_tile_lookup, stored_tile_total
    )
    return activation_matrix[None]


def solution(mesh):
    placed = (
        P("segment", None, "neuron"),
        P(None, None, "neuron"),
        P("segment", None, None, None, "neuron"),
        P("segment", None, "neuron"),
        P("segment", None, None, "neuron"),
        P("segment"),
    )
    return jax.shard_map(
        per_device,
        mesh=mesh,
        in_specs=placed,
        out_specs=P("segment", None, "neuron"),
        check_vma=False,
    )
```

profile of v0, /device:TPU:1, one launch (start us, length us, event | category | flops | bytes accessed | tf_op | source)
XLA Modules:
  0.0 870.3 jit_solution(10240029558922843930)
XLA Ops:
  6.5 2.3 copy.36
  9.6 4.1 fusion.34
  14.5 6.9 reshape_squeeze.8
  22.1 120.2 %all-gather.12.cloned.1.call-done = bf16[1,8,65536]{1,2,0:T(8,128)(2,1)} async-done(((bf16[1,8,4096]{1,2,0:T(8,128)(2,1)}), bf16[1,8,65536]{1,2,0:T(8,128)(2,1)}) %all-gather.12.cloned.1.call-update) | async-done | bytes 1048592 | tf_op jit(solution)/shard_map/all_gather | solution.py:22
  142.3 62.8 %gather_fusion = bf16[16384,8]{1,0:T(8,128)(2,1)} fusion(bf16[8,65536]{0,1:T(8,128)(2,1)} %bitcast.87, s32[16384]{0:T(1024)S(1)} %fusion.32), kind=kCustom, calls=%fused_computation.clone | custom fusion | bytes 589824 | tf_op jit(solution)/shard_map/jit(_take)/gather | solution.py:23
  205.1 11.1 %broadcast_select_fusion.2 = bf16[16384,8]{1,0:T(8,128)(2,1)S(1)} fusion(bf16[16384,8]{1,0:T(8,128)(2,1)} %gather_fusion, pred[16384]{0:T(1024)(128)(4,1)S(1)} %compare_and_fusion.1), kind=kLoop, calls=%fused_computation.6 | loop fusion | flops 131072 | bytes 540672 | tf_op jit(solution)/shard_map/jit(_take)/select_n | solution.py:23
  216.2 4.6 fusion.16
  220.8 2.0 copy.61
  222.8 2.8 fusion.28
  225.9 5.6 reshape_squeeze.9
  231.6 120.6 %all-gather.6.cloned.1.call-done = bf16[8,65536]{0,1:T(8,128)(2,1)} async-done(((bf16[8,4096]{0,1:T(8,128)(2,1)}), bf16[8,65536]{0,1:T(8,128)(2,1)}) %all-gather.6.cloned.1.call-update) | async-done | bytes 1048592 | tf_op jit(solution)/shard_map/all_gather | solution.py:22
  352.2 62.8 %gather_fusion.1 = bf16[16384,8]{1,0:T(8,128)(2,1)} fusion(bf16[8,65536]{0,1:T(8,128)(2,1)} %all-gather.6.cloned.1.call-done, s32[16384]{0:T(1024)S(1)} %fusion.33), kind=kCustom, calls=%fused_computation.1.clone | custom fusion | bytes 589824 | tf_op jit(solution)/shard_map/jit(_take)/gather | solution.py:23
  415.0 11.1 %broadcast_select_fusion = bf16[16384,8]{1,0:T(8,128)(2,1)S(1)} fusion(bf16[16384,8]{1,0:T(8,128)(2,1)} %gather_fusion.1, pred[16384]{0:T(1024)(128)(4,1)S(1)} %compare_and_fusion), kind=kLoop, calls=%fused_computation.4 | loop fusion | flops 131072 | bytes 540672 | tf_op jit(solution)/shard_map/jit(_take)/select_n | solution.py:23
  426.1 4.6 fusion.22
  434.9 3.8 collective-permute-start
  441.9 128.0 %all-gather.8.cloned.1.call-done = bf16[8,65536]{0,1:T(8,128)(2,1)} async-done(((bf16[8,4096]{0,1:T(8,128)(2,1)}), bf16[8,65536]{0,1:T(8,128)(2,1)}) %all-gather.8.cloned.1.call-update) | async-done | bytes 1048592 | tf_op jit(solution)/shard_map/all_gather | solution.py:22
  569.9 62.8 %gather_fusion.2 = bf16[16384,8]{1,0:T(8,128)(2,1)} fusion(bf16[8,65536]{0,1:T(8,128)(2,1)} %all-gather.8.cloned.1.call-done, s32[16384]{0:T(1024)S(1)} %fusion.32), kind=kCustom, calls=%fused_computation.2.clone | custom fusion | bytes 589824 | tf_op jit(solution)/shard_map/jit(_take)/gather | solution.py:23
  632.8 11.1 %broadcast_select_fusion.3 = bf16[16384,8]{1,0:T(8,128)(2,1)S(1)} fusion(bf16[16384,8]{1,0:T(8,128)(2,1)} %gather_fusion.2, pred[16384]{0:T(1024)(128)(4,1)S(1)} %compare_and_fusion.1), kind=kLoop, calls=%fused_computation.7 | loop fusion | flops 131072 | bytes 540672 | tf_op jit(solution)/shard_map/jit(_take)/select_n | solution.py:23
  643.9 4.6 fusion.19
  650.4 2.7 fusion.30
  653.2 126.6 %all-gather.10.cloned.1.call-done = bf16[8,65536]{0,1:T(8,128)(2,1)} async-done(((bf16[8,4096]{0,1:T(8,128)(2,1)}), bf16[8,65536]{0,1:T(8,128)(2,1)}) %all-gather.10.cloned.1.call-update) | async-done | bytes 1048592 | tf_op jit(solution)/shard_map/all_gather | solution.py:22
  779.7 62.8 %gather_fusion.3 = bf16[16384,8]{1,0:T(8,128)(2,1)} fusion(bf16[8,65536]{0,1:T(8,128)(2,1)} %all-gather.10.cloned.1.call-done, s32[16384]{0:T(1024)S(1)} %fusion.33), kind=kCustom, calls=%fused_computation.3.clone | custom fusion | bytes 589824 | tf_op jit(solution)/shard_map/jit(_take)/gather | solution.py:23
  842.5 11.3 %broadcast_select_fusion.1 = bf16[16384,8]{1,0:T(8,128)(2,1)S(1)} fusion(bf16[16384,8]{1,0:T(8,128)(2,1)} %gather_fusion.3, pred[16384]{0:T(1024)(128)(4,1)S(1)} %compare_and_fusion), kind=kLoop, calls=%fused_computation.5 | loop fusion | flops 131072 | bytes 540672 | tf_op jit(solution)/shard_map/jit(_take)/select_n | solution.py:23
  853.9 4.6 fusion.25
  (50 shorter events, 16.3 us)
Async XLA Ops:
  6.5 135.8 %all-gather.12.cloned.1.call-start = ((), (), s32[]{:S(2)}) async-start(), calls=%async_computation.3 | async-start | bytes 17825792 | tf_op jit(solution)/shard_map/all_gather | solution.py:22
  8.8 343.4 %all-gather.6.cloned.1.call-start = ((), (), s32[]{:S(2)}) async-start(), calls=%async_computation | async-start | bytes 17825792 | tf_op jit(solution)/shard_map/all_gather | solution.py:22
  13.6 8.5 copy-start.10
  205.1 11.1 %copy-start = (bf16[4,64,64,64]{3,2,1,0:T(8,128)(2,1)S(1)}, bf16[4,64,64,64]{3,2,1,0:T(8,128)(2,1)}, u32[]{:S(2)}) copy-start(bf16[4,64,64,64]{3,2,1,0:T(8,128)(2,1)} %reshape_squeeze.8) | copy-start | bytes 6291460
  216.2 6.6 copy-start.6
  222.8 3.0 copy-start.8
  225.6 344.4 %all-gather.8.cloned.1.call-start = ((), (), s32[]{:S(2)}) async-start(), calls=%async_computation.1 | async-start | bytes 17825792 | tf_op jit(solution)/shard_map/all_gather | solution.py:22
  415.0 11.1 %copy-start.2 = (bf16[4,64,64,64]{3,2,1,0:T(8,128)(2,1)S(1)}, bf16[4,64,64,64]{3,2,1,0:T(8,128)(2,1)}, u32[]{:S(2)}) copy-start(bf16[4,64,64,64]{3,2,1,0:T(8,128)(2,1)} %reshape_squeeze.9) | copy-start | bytes 6291460
  426.1 6.6 copy-start.4
  430.7 8.0 copy-start.9
  434.9 5.1 collective-permute-start
  441.7 338.1 %all-gather.10.cloned.1.call-start = ((), (), s32[]{:S(2)}) async-start(), calls=%async_computation.2 | async-start | bytes 17825792 | tf_op jit(solution)/shard_map/all_gather | solution.py:22
  632.8 11.1 %copy-start.1 = (bf16[4,64,64,64]{3,2,1,0:T(8,128)(2,1)S(1)}, bf16[4,64,64,64]{3,2,1,0:T(8,128)(2,1)}, u32[]{:S(2)}) copy-start(bf16[4,64,64,64]{3,2,1,0:T(8,128)(2,1)} %reshape_squeeze.8) | copy-start | bytes 6291460
  643.9 6.6 copy-start.7
  842.5 11.3 %copy-start.3 = (bf16[4,64,64,64]{3,2,1,0:T(8,128)(2,1)S(1)}, bf16[4,64,64,64]{3,2,1,0:T(8,128)(2,1)}, u32[]{:S(2)}) copy-start(bf16[4,64,64,64]{3,2,1,0:T(8,128)(2,1)} %reshape_squeeze.9) | copy-start | bytes 6291460
  853.9 6.6 copy-start.5
Sparse Core Ops, SparseCore 0:
  10.4 131.8 all-gather.11
  225.7 126.4 all-gather.5
  441.8 128.1 all-gather.7
  653.3 126.4 all-gather.9
where the time goes:
time: 879 us; the launch traced here: 870 us
  waiting for transfers between devices  496 us (56%)
  local copies, waits for them, and re-layouts  280 us (32%)
  other arithmetic  56.6 us (6%)
  matrix products  18.3 us (2%)
  between operations  14.4 us (2%)
    all_gather x4, waiting for transfers between devices, run_layer(): full = lax.all_gather(y, 'neuron', axis=1, tiled=True)  495 us
    gather x4, local copies, waits for them, and re-layouts, run_layer(): jnp.take(full, cols.reshape(-1), axis=1).reshape(rows, KB, blocks_here, BLK)  251 us
    select_n x4, other arithmetic, run_layer(): jnp.take(full, cols.reshape(-1), axis=1).reshape(rows, KB, blocks_here, BLK)  44.6 us
    dot_general x4, matrix products, run_layer(): jnp.einsum('bkjr,krjc->bjc', taken, w_blocks, preferred_element_type=jnp....  18.3 us
  transfers between devices with their start and end apart: 5, of which 5 were waited for; matrix products, arithmetic and copies ran while one was open for 2% of the time, Pallas kernels for 0%

commit v1 on v0

v1 whole, which is shorter than its diff:
```python
import functools

import jax
import jax.numpy as jnp
from jax import lax
from jax.experimental import pallas as pl
from jax.experimental.pallas import tpu as pltpu
from jax.sharding import PartitionSpec as P

BLK = 64
KB = 4
LMAX = 2
STAGES = 4
LANES = 128
SIDE = 4
MESH = pl.DeviceIdType.MESH


def torus_distance(step):
    return sum(min(c, SIDE - c) for c in step)


STEPS_FAR = sorted(
    ((dy, dx) for dy in range(SIDE) for dx in range(SIDE)), key=lambda s: -torus_distance(s)
)
STEPS_NEAR = sorted(
    ((dy, dx) for dy in range(SIDE) for dx in range(SIDE)), key=torus_distance
)


def lists_of_blocks(idx_ref, shards, per_source):
    rows = LMAX * KB
    per_shard = idx_ref.shape[-1]
    shard = lax.broadcasted_iota(jnp.int32, (shards, per_shard), 0)
    place = lax.broadcasted_iota(jnp.int32, (LANES, per_shard), 0)
    before = (
        lax.broadcasted_iota(jnp.int32, (per_shard, per_shard), 0)
        < lax.broadcasted_iota(jnp.int32, (per_shard, per_shard), 1)
    ).astype(jnp.bfloat16)
    entries = [idx_ref[0, r // KB, pl.ds(r % KB, 1), :] for r in range(rows)]
    sources = [e // per_shard for e in entries]
    masks = [(jnp.broadcast_to(s, shard.shape) == shard).astype(jnp.float32) for s in sources]
    ahead = jnp.dot(
        jnp.concatenate(masks, axis=0).astype(jnp.bfloat16),
        before,
        preferred_element_type=jnp.float32,
    )
    wanted = jnp.zeros((shards, LANES), jnp.float32)
    slots = []
    for level in range(LMAX):
        count = jnp.zeros((shards, 1), jnp.float32)
        for k in range(KB):
            r = level * KB + k
            mask = masks[r]
            rank = jnp.sum(
                mask * (ahead[r * shards : (r + 1) * shards] + count), axis=0, keepdims=True
            ).astype(jnp.int32)
            rank = jnp.clip(rank, 0, per_source - 1)
            side, pair = rank & 1, rank >> 1
            count = count + jnp.sum(mask, axis=1, keepdims=True)
            tile = sources[r] * (per_source // 2) + pair
            slots.append(tile + (side ^ (k & 1)) * (shards * per_source // 2))
            local = entries[r] & (per_shard - 1)
            local = ((local >> 1) + ((local ^ rank) & 1) * (per_shard // 2)).astype(jnp.float32)
            chosen = (mask * local).astype(jnp.bfloat16)
            placed = (
                jnp.broadcast_to(rank + level * per_source, place.shape) == place
            ).astype(jnp.bfloat16)
            wanted = wanted + lax.dot_general(
                chosen, placed, (((1,), (1,)), ((), ())), preferred_element_type=jnp.float32
            )
    return jnp.clip(wanted.astype(jnp.int32), 0, per_shard - 1), slots


def kernel(
    segments,
    shards,
    depth_ref,
    pending_ref,
    arriving_ref,
    weight_ref,
    offset_ref,
    idx_ref,
    out_ref,
    weights,
    own,
    send,
    recv,
    table,
    bias,
    entering,
    wants,
    arrived,
    slot_vmem,
    lists,
    slots,
    weight_sem,
    slot_sem,
    row_sem,
    list_send_sem,
    list_sem,
    next_send_sem,
    next_sem,
    send_sem,
    recv_sem,
):
    seg = lax.axis_index("segment")
    me = lax.axis_index("neuron")
    after = lax.rem(seg + 1, segments)
    ahead = lax.rem(seg + segments - 1, segments)
    row, col = lax.div(me, SIDE), lax.rem(me, SIDE)

    def peer(step):
        return lax.rem(row + step[0], SIDE) * SIDE + lax.rem(col + step[1], SIDE)

    far = [peer(s) for s in STEPS_FAR]
    near = [peer(s) for s in STEPS_NEAR]
    blocks = idx_ref.shape[-1]
    per_source = KB * blocks // shards
    tall = per_source * 4
    column_tiles = weights.shape[1]
    pairs = column_tiles
    low = lax.broadcasted_iota(jnp.int32, (8, LANES), 1) < BLK

    barrier = pltpu.get_barrier_semaphore()
    for p in far[:-1]:
        pl.semaphore_signal(barrier, inc=1, device_id=(seg, p), device_id_type=MESH)
    pl.semaphore_signal(barrier, inc=1, device_id=(after, me), device_id_type=MESH)
    pl.semaphore_signal(barrier, inc=1, device_id=(ahead, me), device_id_type=MESH)

    def weight_copy(level, c):
        return pltpu.make_async_copy(
            weight_ref.at[0, level, :, :, pl.ds(pl.multiple_of(c * LANES, LANES), LANES)],
            weights.at[level, c],
            weight_sem.at[level],
        )

    for level in range(LMAX):

        @pl.loop(0, column_tiles)
        def _(c):
            weight_copy(level, c).start()

    wanted, landing = lists_of_blocks(idx_ref, shards, per_source)
    for v in range(shards):
        wants[v] = wanted[v : v + 1]
    for r in range(LMAX * KB):
        slot_vmem[r, :, pl.ds(0, blocks)] = landing[r]
    slot_copy = pltpu.make_async_copy(slot_vmem, slots, slot_sem)
    slot_copy.start()

    def keep(tiles):
        tiles = tiles.reshape(pairs, 8, LANES)
        own[pl.ds(0, pairs)] = tiles
        own[pl.ds(pairs, pairs)] = pltpu.roll(tiles, BLK, 2)

    def tiles_of(ref):
        return jnp.concatenate(
            [ref[0, :, pl.ds(p * LANES, LANES)] for p in range(pairs)], axis=0
        ).astype(jnp.float32)

    for level in range(LMAX):
        for p in range(pairs):
            bias[level, p] = offset_ref[0, pl.ds(level, 1), pl.ds(p * LANES, LANES)]
    entering[...] = tiles_of(arriving_ref)
    keep(tiles_of(pending_ref))

    pl.semaphore_wait(barrier, len(far) + 1)

    def list_copy(p):
        return pltpu.make_async_remote_copy(
            src_ref=wants.at[p],
            dst_ref=arrived.at[me],
            send_sem=list_send_sem,
            recv_sem=list_sem.at[me],
            device_id=(seg, p),
            device_id_type=MESH,
        )

    for p in far[:-1]:
        list_copy(p).start()
    pltpu.make_async_copy(wants.at[me], arrived.at[me], list_sem.at[me]).start()

    def row_copy(p):
        return pltpu.make_async_copy(arrived.at[p], lists.at[p], row_sem.at[p])

    def list_take(p):
        pltpu.make_async_copy(wants.at[p], arrived.at[p], list_sem.at[p]).wait()
        row_copy(p).start()

    def gather_for(t, level, first_row, p):
        at = level * per_source
        row = first_row + p
        even, odd = (
            jnp.concatenate([own[lists[row, 0, at + 2 * q + h]] for q in range(per_source // 2)], axis=0)
            for h in range(2)
        )
        side = jnp.concatenate([low] * (per_source // 2), axis=0)
        send[t, block_rows(p), :] = jnp.where(side, even, odd).astype(jnp.bfloat16)

    def block_rows(p):
        return pl.ds(pl.multiple_of(p * tall, tall), tall)

    def data_copy(t, s, p):
        return pltpu.make_async_remote_copy(
            src_ref=send.at[t, block_rows(p)],
            dst_ref=recv.at[t, block_rows(me)],
            send_sem=send_sem.at[t],
            recv_sem=recv_sem.at[t],
            device_id=(s, p),
            device_id_type=MESH,
        )

    depth = depth_ref[0]

    def run(t):
        level = t % 2
        across = t == 2
        first_row = shards if across else 0
        s = after if across else seg
        order = near if t == 0 else far
        if across:
            later = pl.ds(shards, shards)
            pltpu.make_async_copy(wants, arrived.at[later], next_sem).wait()
            every = pltpu.make_async_copy(arrived.at[later], lists.at[later], slot_sem)
            every.start()
            every.wait()
        if t == 0:
            for p in order:
                list_take(p)
        for i, p in enumerate(order):
            local = STEPS_NEAR[i] == (0, 0) if t == 0 else STEPS_FAR[i] == (0, 0)
            if t == 0:
                row_copy(p).wait()
            gather_for(t, level, first_row, p)
            if local and not across:
                pltpu.make_async_copy(
                    send.at[t, block_rows(p)], recv.at[t, block_rows(p)], recv_sem.at[t]
                ).start()
            else:
                data_copy(t, s, p).start()
        if t == 0:
            for p in far:
                pltpu.make_async_remote_copy(
                    src_ref=wants.at[p],
                    dst_ref=arrived.at[shards + me],
                    send_sem=next_send_sem,
                    recv_sem=next_sem,
                    device_id=(ahead, p),
                    device_id_type=MESH,
                ).start()
            slot_copy.wait()
        if t < 2:
            pltpu.make_async_copy(
                weight_ref.at[0, level],
                weight_ref.at[0, level],
                weight_sem.at[level],
            ).wait()
        pltpu.make_async_copy(send.at[t], recv.at[t], recv_sem.at[t]).wait()
        half = shards * per_source // 2
        for v in range(shards):
            got = recv[t, pl.ds(v * tall, tall), :].astype(jnp.float32)
            got = got.reshape(per_source // 2, 8, LANES)
            table[pl.ds(v * (per_source // 2), per_source // 2)] = got
            table[pl.ds(half + v * (per_source // 2), per_source // 2)] = pltpu.roll(got, BLK, 2)
        side = jnp.concatenate([low] * 4, axis=0)
        fresh = []
        for c in range(column_tiles // 2):
            left = []
            for pair in range(KB // 2):
                a, b = (
                    jnp.concatenate(
                        [table[slots[level * KB + 2 * pair + h, 0, 4 * c + j]] for j in range(4)], axis=0
                    )
                    for h in range(2)
                )
                left.append(jnp.where(side, a, b))
            left = jnp.concatenate(left, axis=1).astype(jnp.bfloat16)
            right = jnp.concatenate(
                [weights[level, 2 * c + i].reshape(KB * BLK, LANES) for i in range(2)], axis=1
            )
            total = jnp.dot(left, right, preferred_element_type=jnp.float32)
            fresh.append(jnp.where(low, total[0:8, 0:LANES], total[8:16, 0:LANES]))
            fresh.append(jnp.where(low, total[16:24, LANES:], total[24:32, LANES:]))
        fresh = jnp.concatenate(fresh, axis=0).reshape(pairs, 8, LANES) + bias[level]
        fresh = jnp.clip(fresh, 0.0, 32.0).astype(jnp.bfloat16).astype(jnp.float32)
        if level > 0:
            fresh = jnp.where(depth > level, fresh, own[pl.ds(0, pairs)])
        if t == 1:
            fresh = jnp.where(seg == segments - 1, entering[...].reshape(fresh.shape), fresh)
        if t < STAGES - 1:
            keep(fresh)
        else:
            for p in range(pairs):
                out_ref[0, :, pl.ds(p * LANES, LANES)] = fresh[p].astype(jnp.bfloat16)

    for t in range(STAGES):
        run(t)

    some = pl.ds(0, (shards - 1) * tall)
    for t in range(STAGES):
        rows = pl.ds(0, shards * tall) if t == 2 else some
        pltpu.make_async_copy(send.at[t, rows], recv.at[t, rows], send_sem.at[t]).wait()
    pltpu.make_async_copy(
        wants.at[pl.ds(0, shards - 1)], arrived.at[pl.ds(0, shards - 1)], list_send_sem
    ).wait()
    pltpu.make_async_copy(wants, arrived.at[pl.ds(0, shards)], next_send_sem).wait()


def solution(mesh):
    segments, shards = mesh.shape["segment"], mesh.shape["neuron"]

    def per_device(pending, arriving, coefficients, offsets, lookup, depth):
        rows, wide = pending.shape[1:]
        blocks = lookup.shape[-1]
        per_source = KB * blocks // shards
        tall = per_source * 4
        vmem = pl.BlockSpec(memory_space=pltpu.VMEM)
        return pl.pallas_call(
            functools.partial(kernel, segments, shards),
            out_shape=jax.ShapeDtypeStruct(pending.shape, jnp.bfloat16),
            in_specs=[
                pl.BlockSpec(memory_space=pltpu.SMEM),
                vmem,
                vmem,
                pl.BlockSpec(memory_space=pl.ANY),
                vmem,
                vmem,
            ],
            out_specs=vmem,
            scratch_shapes=[
                pltpu.VMEM((LMAX, wide // LANES, KB, BLK, LANES), jnp.bfloat16),
                pltpu.VMEM((blocks, rows, LANES), jnp.float32),
                pltpu.VMEM((STAGES, shards * tall, LANES), jnp.bfloat16),
                pltpu.VMEM((STAGES, shards * tall, LANES), jnp.bfloat16),
                pltpu.VMEM((shards * per_source, rows, LANES), jnp.float32),
                pltpu.VMEM((LMAX, wide // LANES, 1, LANES), jnp.float32),
                pltpu.VMEM((wide // LANES * rows, LANES), jnp.float32),
                pltpu.VMEM((shards, 1, LANES), jnp.int32),
                pltpu.VMEM((2 * shards, 1, LANES), jnp.int32),
                pltpu.VMEM((LMAX * KB, 1, LANES), jnp.int32),
                pltpu.SMEM((2 * shards, 1, LANES), jnp.int32),
                pltpu.SMEM((LMAX * KB, 1, LANES), jnp.int32),
                pltpu.SemaphoreType.DMA((LMAX,)),
                pltpu.SemaphoreType.DMA,
                pltpu.SemaphoreType.DMA((shards,)),
                pltpu.SemaphoreType.DMA,
                pltpu.SemaphoreType.DMA((shards,)),
                pltpu.SemaphoreType.DMA,
                pltpu.SemaphoreType.DMA,
                pltpu.SemaphoreType.DMA((STAGES,)),
                pltpu.SemaphoreType.DMA((STAGES,)),
            ],
            compiler_params=pltpu.CompilerParams(
                collective_id=0, has_side_effects=True, vmem_limit_bytes=32 * 1024 * 1024
            ),
        )(depth, pending, arriving, coefficients, offsets, lookup)

    placed = (
        P("segment", None, "neuron"),
        P(None, None, "neuron"),
        P("segment", None, None, None, "neuron"),
        P("segment", None, "neuron"),
        P("segment", None, None, "neuron"),
        P("segment"),
    )
    return jax.shard_map(
        per_device,
        mesh=mesh,
        in_specs=placed,
        out_specs=P("segment", None, "neuron"),
        check_vma=False,
    )
```

time: 879 us -> 51.4 us (0.06)
  waiting for transfers between devices: 496 us -> 0 us
  local copies, waits for them, and re-layouts: 280 us -> 5.93 us
  other arithmetic: 56.6 us -> 0 us
  Pallas kernels: 0 us -> 44.5 us
  matrix products: 18.3 us -> 0 us
  between operations: 14.4 us -> 0.67 us
    all_gather x4 -> x0, waiting for transfers between devices: 495 us -> none  [run_layer(): full = lax.all_gather(y, 'neuron', axis=1, tiled=True)]
    gather x4 -> x0, local copies, waits for them, and re-layouts: 251 us -> none  [run_layer(): jnp.take(full, cols.reshape(-1), axis=1).reshape(rows, KB, blocks_here, BLK)]
    select_n x9 -> x0, other arithmetic: 55.1 us -> none  [the longest x4 44.6 us: run_layer(): jnp.take(full, cols.reshape(-1), axis=1).reshape(rows, KB, blocks_here, BLK)]
    pallas_call x0 -> x1, Pallas kernels: none -> 44.5 us  [per_device(): pl.pallas_call(functools.partial(kernel, segments, shards), out_shape=jax...]
    dot_general x4 -> x0, matrix products: 18.3 us -> none  [run_layer(): jnp.einsum('bkjr,krjc->bjc', taken, w_blocks, preferred_element_type=jnp....]
    another operation x2 -> x0, local copies, waits for them, and re-layouts: 12.5 us -> none  [run_layer(): w_blocks = w.reshape(KB, BLK, blocks_here, BLK)]
  transfers between devices with their start and end apart: 5 -> 0, of which waited for: 5 -> 0; matrix products, arithmetic and copies ran while one was open for 2% -> 0% of each run, Pallas kernels for 0% -> 0%
where the time goes in v1:
time: 51.4 us; the launch traced here: 51.1 us
  Pallas kernels  44.5 us (87%)
  local copies, waits for them, and re-layouts  5.93 us (12%)
  between operations  0.67 us (1%)
    pallas_call x1, Pallas kernels, per_device(): pl.pallas_call(functools.partial(kernel, segments, shards), out_shape=jax...  44.5 us
    unnamed x11, local copies, waits for them, and re-layouts  5.93 us

profile of v1, /device:TPU:1, one launch (start us, length us, event | category | flops | bytes accessed | tf_op | source)
XLA Modules:
  0.0 51.1 jit_solution(4998462745680099094)
XLA Ops:
  0.7 0.0 copy-start
  0.7 2.2 %copy-done = bf16[1,2,4,64,4096]{4,3,2,1,0:T(8,128)(2,1)S(1)} copy-done((bf16[1,2,4,64,4096]{4,3,2,1,0:T(8,128)(2,1)S(1)}, bf16[1,2,4,64,4096]{4,3,2,1,0:T(8,128)(2,1)}, u32[]{:S(2)}) %copy-start) | copy-done | bytes 4194328
  2.8 0.0 copy-start.1
  2.8 0.8 %copy-done.1 = bf16[1,8,4096]{2,1,0:T(8,128)(2,1)S(1)} copy-done((bf16[1,8,4096]{2,1,0:T(8,128)(2,1)S(1)}, bf16[1,8,4096]{2,1,0:T(8,128)(2,1)}, u32[]{:S(2)}) %copy-start.1) | copy-done | bytes 65560
  3.7 0.0 copy-start.2
  3.7 0.8 %copy-done.2 = bf16[1,8,4096]{2,1,0:T(8,128)(2,1)S(1)} copy-done((bf16[1,8,4096]{2,1,0:T(8,128)(2,1)S(1)}, bf16[1,8,4096]{2,1,0:T(8,128)(2,1)}, u32[]{:S(2)}) %copy-start.2) | copy-done | bytes 65560
  4.5 0.0 copy-start.3
  4.5 0.8 %copy-done.3 = f32[1,2,4096]{2,1,0:T(2,128)S(1)} copy-done((f32[1,2,4096]{2,1,0:T(2,128)S(1)}, f32[1,2,4096]{2,1,0:T(2,128)}, u32[]{:S(2)}) %copy-start.3) | copy-done | bytes 32792
  5.3 0.0 copy-start.4
  5.3 0.7 %copy-done.4 = s32[1,2,4,64]{3,2,1,0:T(4,128)S(1)} copy-done((s32[1,2,4,64]{3,2,1,0:T(4,128)S(1)}, s32[1,2,4,64]{3,2,1,0:T(4,128)}, u32[]{:S(2)}) %copy-start.4) | copy-done | bytes 2072
  6.0 44.5 %shard_map.64 = bf16[1,8,4096]{2,1,0:T(8,128)(2,1)S(1)} custom-call(s32[1]{0:T(128)S(6)} %copy.8.depth_ref, bf16[1,8,4096]{2,1,0:T(8,128)(2,1)S(1)} %copy-done.1, bf16[1,8,4096]{2,1,0:T(8,128)(2,1)S(1)} %copy-done.2, bf16[1,2,4,64,4096]{4,3,2,1,0:T(8,128)(2,1)S(1)} %copy-done, f32[1,2,4096]{2,1,0:T(2,128)S(1)} %copy-done.3, s32[1,2,4,64]{3,2,1,0:T(4,128)S(1)} %copy-done.4), custom_call_target="tpu_custom_call" | custom-call | tf_op jit(solution)/shard_map/pallas_call | solution.py:319
  50.5 0.6 %copy.9 = bf16[1,8,4096]{2,1,0:T(8,128)(2,1)} copy(bf16[1,8,4096]{2,1,0:T(8,128)(2,1)S(1)} %shard_map.64) | data formatting | bytes 131072
Async XLA Ops:
  0.7 2.2 %copy-start = (bf16[1,2,4,64,4096]{4,3,2,1,0:T(8,128)(2,1)S(1)}, bf16[1,2,4,64,4096]{4,3,2,1,0:T(8,128)(2,1)}, u32[]{:S(2)}) copy-start(bf16[1,2,4,64,4096]{4,3,2,1,0:T(8,128)(2,1)} %weight_ref.1) | copy-start | bytes 12582916
  2.8 0.8 %copy-start.1 = (bf16[1,8,4096]{2,1,0:T(8,128)(2,1)S(1)}, bf16[1,8,4096]{2,1,0:T(8,128)(2,1)}, u32[]{:S(2)}) copy-start(bf16[1,8,4096]{2,1,0:T(8,128)(2,1)} %pending_ref.1) | copy-start | bytes 196612
  3.7 0.8 %copy-start.2 = (bf16[1,8,4096]{2,1,0:T(8,128)(2,1)S(1)}, bf16[1,8,4096]{2,1,0:T(8,128)(2,1)}, u32[]{:S(2)}) copy-start(bf16[1,8,4096]{2,1,0:T(8,128)(2,1)} %arriving_ref.1) | copy-start | bytes 196612
  4.5 0.8 %copy-start.3 = (f32[1,2,4096]{2,1,0:T(2,128)S(1)}, f32[1,2,4096]{2,1,0:T(2,128)}, u32[]{:S(2)}) copy-start(f32[1,2,4096]{2,1,0:T(2,128)} %offset_ref.1) | copy-start | bytes 98308
  5.3 0.7 %copy-start.4 = (s32[1,2,4,64]{3,2,1,0:T(4,128)S(1)}, s32[1,2,4,64]{3,2,1,0:T(4,128)}, u32[]{:S(2)}) copy-start(s32[1,2,4,64]{3,2,1,0:T(4,128)} %idx_ref.1) | copy-start | bytes 6148

commit v2 on v1

v2 whole, which is shorter than its diff:
```python
import functools

import jax
import jax.numpy as jnp
from jax import lax
from jax.experimental import pallas as pl
from jax.experimental.pallas import tpu as pltpu
from jax.sharding import PartitionSpec as P

BLK = 64
KB = 4
LMAX = 2
STAGES = 4
NEAR = 11
LANES = 128
SIDE = 4
MESH = pl.DeviceIdType.MESH


def torus_distance(step):
    return sum(min(c, SIDE - c) for c in step)


STEPS_FAR = sorted(
    ((dy, dx) for dy in range(SIDE) for dx in range(SIDE)), key=lambda s: -torus_distance(s)
)
STEPS_NEAR = sorted(
    ((dy, dx) for dy in range(SIDE) for dx in range(SIDE)), key=torus_distance
)


def lists_of_blocks(idx_ref, shards, per_source):
    rows = LMAX * KB
    per_shard = idx_ref.shape[-1]
    shard = lax.broadcasted_iota(jnp.int32, (shards, per_shard), 0)
    place = lax.broadcasted_iota(jnp.int32, (LANES, per_shard), 0)
    before = (
        lax.broadcasted_iota(jnp.int32, (per_shard, per_shard), 0)
        < lax.broadcasted_iota(jnp.int32, (per_shard, per_shard), 1)
    ).astype(jnp.bfloat16)
    entries = [idx_ref[0, r // KB, pl.ds(r % KB, 1), :] for r in range(rows)]
    sources = [e // per_shard for e in entries]
    masks = [(jnp.broadcast_to(s, shard.shape) == shard).astype(jnp.float32) for s in sources]
    ahead = jnp.dot(
        jnp.concatenate(masks, axis=0).astype(jnp.bfloat16),
        before,
        preferred_element_type=jnp.float32,
    )
    wanted = jnp.zeros((shards, LANES), jnp.float32)
    slots = []
    for level in range(LMAX):
        count = jnp.zeros((shards, 1), jnp.float32)
        for k in range(KB):
            r = level * KB + k
            mask = masks[r]
            rank = jnp.sum(
                mask * (ahead[r * shards : (r + 1) * shards] + count), axis=0, keepdims=True
            ).astype(jnp.int32)
            rank = jnp.clip(rank, 0, per_source - 1)
            side, pair = rank & 1, rank >> 1
            count = count + jnp.sum(mask, axis=1, keepdims=True)
            tile = sources[r] * (per_source // 2) + pair
            slots.append(tile + (side ^ (k & 1)) * (shards * per_source // 2))
            local = entries[r] & (per_shard - 1)
            local = ((local >> 1) + ((local ^ rank) & 1) * (per_shard // 2)).astype(jnp.float32)
            chosen = (mask * local).astype(jnp.bfloat16)
            placed = (
                jnp.broadcast_to(rank + level * per_source, place.shape) == place
            ).astype(jnp.bfloat16)
            wanted = wanted + lax.dot_general(
                chosen, placed, (((1,), (1,)), ((), ())), preferred_element_type=jnp.float32
            )
    return jnp.clip(wanted.astype(jnp.int32), 0, per_shard - 1), slots


def kernel(
    segments,
    shards,
    depth_ref,
    pending_ref,
    arriving_ref,
    weight_ref,
    offset_ref,
    idx_ref,
    out_ref,
    pending,
    arriving,
    offsets,
    idx,
    weights,
    own,
    entering,
    send,
    send_entering,
    recv,
    table,
    bias,
    wants,
    arrived,
    slot_vmem,
    lists,
    slots,
    load_sem,
    weight_sem,
    slot_sem,
    row_sem,
    list_send_sem,
    list_sem,
    next_send_sem,
    next_sem,
    next_here,
    send_sem,
    send_entering_sem,
    recv_sem,
):
    seg = lax.axis_index("segment")
    me = lax.axis_index("neuron")
    first, last = seg == 0, seg == segments - 1
    after = lax.rem(seg + 1, segments)
    ahead = lax.rem(seg + segments - 1, segments)
    row, col = lax.div(me, SIDE), lax.rem(me, SIDE)

    def peer(step):
        return lax.rem(row + step[0], SIDE) * SIDE + lax.rem(col + step[1], SIDE)

    far = [peer(s) for s in STEPS_FAR]
    near = [peer(s) for s in STEPS_NEAR]
    blocks = idx_ref.shape[-1]
    per_source = KB * blocks // shards
    tall = per_source * 4
    column_tiles = weights.shape[-1] // LANES
    pairs = column_tiles
    low = lax.broadcasted_iota(jnp.int32, (8, LANES), 1) < BLK

    load = [
        pltpu.make_async_copy(source, target, load_sem.at[i])
        for i, (source, target) in enumerate(
            ((idx_ref, idx), (pending_ref, pending), (offset_ref, offsets), (arriving_ref, arriving))
        )
    ]
    load[0].start()
    barrier = pltpu.get_barrier_semaphore()
    for p in far[:-1]:
        pl.semaphore_signal(barrier, inc=1, device_id=(seg, p), device_id_type=MESH)

    @pl.when(jnp.logical_not(last))
    def _():
        pl.semaphore_signal(barrier, inc=1, device_id=(after, me), device_id_type=MESH)

    for copy in load[1:]:
        copy.start()

    load[0].wait()
    wanted, landing = lists_of_blocks(idx, shards, per_source)
    for v in range(shards):
        wants[v] = wanted[v : v + 1]

    pl.semaphore_wait(barrier, jnp.where(first, shards - 1, shards))

    def list_copy(p):
        return pltpu.make_async_remote_copy(
            src_ref=wants.at[p],
            dst_ref=arrived.at[me],
            send_sem=list_send_sem,
            recv_sem=list_sem.at[me],
            device_id=(seg, p),
            device_id_type=MESH,
        )

    for p in far[:-1]:
        list_copy(p).start()
    pltpu.make_async_copy(wants.at[me], arrived.at[me], list_sem.at[me]).start()

    @pl.when(jnp.logical_not(first))
    def _():
        pl.semaphore_signal(next_here, inc=1, device_id=(ahead, me), device_id_type=MESH)

    for r in range(LMAX * KB):
        slot_vmem[r, :, pl.ds(0, blocks)] = landing[r]
    slot_copy = pltpu.make_async_copy(slot_vmem, slots, slot_sem)
    slot_copy.start()

    for level in range(LMAX):
        pltpu.make_async_copy(
            weight_ref.at[0, level], weights.at[level], weight_sem.at[level]
        ).start()

    def keep(tiles, where):
        tiles = tiles.reshape(pairs, 8, LANES)
        where[pl.ds(0, pairs)] = tiles
        where[pl.ds(pairs, pairs)] = pltpu.roll(tiles, BLK, 2)

    def tiles_of(ref):
        return jnp.concatenate(
            [ref[0, :, pl.ds(p * LANES, LANES)] for p in range(pairs)], axis=0
        ).astype(jnp.float32)

    load[1].wait()
    keep(tiles_of(pending), own)
    load[2].wait()
    for level in range(LMAX):
        for p in range(pairs):
            bias[level, p] = offsets[0, pl.ds(level, 1), pl.ds(p * LANES, LANES)]

    def row_copy(p):
        return pltpu.make_async_copy(arrived.at[p], lists.at[p], row_sem.at[p])

    def list_take(p):
        pltpu.make_async_copy(wants.at[p], arrived.at[p], list_sem.at[p]).wait()
        row_copy(p).start()

    def gather_for(where, level, row, target, p):
        at = level * per_source
        even, odd = (
            jnp.concatenate(
                [where[lists[row, 0, at + 2 * q + h]] for q in range(per_source // 2)], axis=0
            )
            for h in range(2)
        )
        side = jnp.concatenate([low] * (per_source // 2), axis=0)
        target[block_rows(p), :] = jnp.where(side, even, odd).astype(jnp.bfloat16)

    def block_rows(p):
        return pl.ds(pl.multiple_of(p * tall, tall), tall)

    def give(t, s, p, source, sem, local):
        if local:
            pltpu.make_async_copy(
                source.at[block_rows(p)], recv.at[t, block_rows(p)], recv_sem.at[t, me]
            ).start()
            return
        pltpu.make_async_remote_copy(
            src_ref=source.at[block_rows(p)],
            dst_ref=recv.at[t, block_rows(me)],
            send_sem=sem,
            recv_sem=recv_sem.at[t, me],
            device_id=(s, p),
            device_id_type=MESH,
        ).start()

    depth = depth_ref[0]

    def send_first():
        def one(i):
            row_copy(near[i]).wait()
            gather_for(own, 0, near[i], send.at[0], near[i])
            give(0, seg, near[i], send.at[0], send_sem.at[0], i == 0)

        for group in (range(NEAR), range(NEAR, shards)):
            for i in group:
                list_take(near[i])
            for i in reversed(group):
                one(i)

        @pl.when(jnp.logical_not(first))
        def _():
            for p in far:
                pltpu.make_async_remote_copy(
                    src_ref=wants.at[p],
                    dst_ref=arrived.at[shards + me],
                    send_sem=next_send_sem,
                    recv_sem=next_sem,
                    device_id=(ahead, p),
                    device_id_type=MESH,
                ).start()

        load[3].wait()

        @pl.when(first)
        def _():
            keep(tiles_of(arriving), entering)
            for i, p in enumerate(far):
                gather_for(entering, 0, p, send_entering, p)
                give(2, seg, p, send_entering, send_entering_sem, i == shards - 1)

        slot_copy.wait()

    def send_within(t):
        for i, p in enumerate(far):
            gather_for(own, t % LMAX, p, send.at[t], p)
            give(t, seg, p, send.at[t], send_sem.at[t], i == shards - 1)

    def send_across(t):
        @pl.when(jnp.logical_not(last))
        def _():
            later = pl.ds(shards, shards)
            pltpu.make_async_copy(wants, arrived.at[later], next_sem).wait()
            every = pltpu.make_async_copy(arrived.at[later], lists.at[later], slot_sem)
            every.start()
            pl.semaphore_wait(next_here, 1)
            every.wait()
            for p in far:
                gather_for(own, 0, shards + p, send.at[t], p)
                give(t, after, p, send.at[t], send_sem.at[t], False)

    def apply(t):
        level = t % LMAX
        if t < LMAX:
            pltpu.make_async_copy(
                weight_ref.at[0, level], weight_ref.at[0, level], weight_sem.at[level]
            ).wait()
        half = shards * per_source // 2
        deep = per_source // 2
        for group in (near[:NEAR], near[NEAR:]):
            for v in group:
                pltpu.make_async_copy(
                    send.at[t, block_rows(v)], recv.at[t, block_rows(v)], recv_sem.at[t, v]
                ).wait()
            for v in group:
                got = recv[t, block_rows(v), :].astype(jnp.float32).reshape(deep, 8, LANES)
                table[pl.ds(v * deep, deep)] = got
                table[pl.ds(half + v * deep, deep)] = pltpu.roll(got, BLK, 2)
        side = jnp.concatenate([low] * 4, axis=0)
        fresh = []
        for c in range(column_tiles // 2):
            left = []
            for pair in range(KB // 2):
                a, b = (
                    jnp.concatenate(
                        [table[slots[level * KB + 2 * pair + h, 0, 4 * c + j]] for j in range(4)], axis=0
                    )
                    for h in range(2)
                )
                left.append(jnp.where(side, a, b))
            left = jnp.concatenate(left, axis=1).astype(jnp.bfloat16)
            right = weights[level, :, :, pl.ds(2 * c * LANES, 2 * LANES)]
            right = right.reshape(KB * BLK, 2 * LANES)
            total = jnp.dot(left, right, preferred_element_type=jnp.float32)
            fresh.append(jnp.where(low, total[0:8, 0:LANES], total[8:16, 0:LANES]))
            fresh.append(jnp.where(low, total[16:24, LANES:], total[24:32, LANES:]))
        fresh = jnp.concatenate(fresh, axis=0).reshape(pairs, 8, LANES) + bias[level]
        fresh = jnp.clip(fresh, 0.0, 32.0).astype(jnp.bfloat16).astype(jnp.float32)
        if level > 0:
            fresh = jnp.where(depth > level, fresh, own[pl.ds(0, pairs)])
        if t < STAGES - 1:
            keep(fresh, own)
        else:
            for p in range(pairs):
                out_ref[0, :, pl.ds(p * LANES, LANES)] = fresh[p].astype(jnp.bfloat16)

    send_first()
    apply(0)
    send_within(1)
    apply(1)
    send_across(2)
    apply(2)
    send_within(3)
    apply(3)

    def settle(rows, sem):
        pltpu.make_async_copy(send.at[0, rows], recv.at[0, rows], sem).wait()

    some, whole = pl.ds(0, (shards - 1) * tall), pl.ds(0, shards * tall)
    for t in (0, 1, 3):
        settle(some, send_sem.at[t])

    @pl.when(jnp.logical_not(last))
    def _():
        settle(whole, send_sem.at[2])

    @pl.when(first)
    def _():
        settle(some, send_entering_sem)

    pltpu.make_async_copy(
        wants.at[pl.ds(0, shards - 1)], arrived.at[pl.ds(0, shards - 1)], list_send_sem
    ).wait()

    @pl.when(jnp.logical_not(first))
    def _():
        pltpu.make_async_copy(wants, arrived.at[pl.ds(0, shards)], next_send_sem).wait()


def solution(mesh):
    segments, shards = mesh.shape["segment"], mesh.shape["neuron"]

    def per_device(pending, arriving, coefficients, offsets, lookup, depth):
        rows, wide = pending.shape[1:]
        blocks = lookup.shape[-1]
        per_source = KB * blocks // shards
        tall = per_source * 4
        pairs = wide // LANES
        anywhere = pl.BlockSpec(memory_space=pl.ANY)
        return pl.pallas_call(
            functools.partial(kernel, segments, shards),
            out_shape=jax.ShapeDtypeStruct(pending.shape, jnp.bfloat16),
            in_specs=[pl.BlockSpec(memory_space=pltpu.SMEM)] + [anywhere] * 5,
            out_specs=pl.BlockSpec(memory_space=pltpu.VMEM),
            scratch_shapes=[
                pltpu.VMEM(pending.shape, jnp.bfloat16),
                pltpu.VMEM(arriving.shape, jnp.bfloat16),
                pltpu.VMEM(offsets.shape, jnp.float32),
                pltpu.VMEM(lookup.shape, jnp.int32),
                pltpu.VMEM((LMAX, KB, BLK, wide), jnp.bfloat16),
                pltpu.VMEM((blocks, rows, LANES), jnp.float32),
                pltpu.VMEM((blocks, rows, LANES), jnp.float32),
                pltpu.VMEM((STAGES, shards * tall, LANES), jnp.bfloat16),
                pltpu.VMEM((shards * tall, LANES), jnp.bfloat16),
                pltpu.VMEM((STAGES, shards * tall, LANES), jnp.bfloat16),
                pltpu.VMEM((shards * per_source, rows, LANES), jnp.float32),
                pltpu.VMEM((LMAX, pairs, 1, LANES), jnp.float32),
                pltpu.VMEM((shards, 1, LANES), jnp.int32),
                pltpu.VMEM((2 * shards, 1, LANES), jnp.int32),
                pltpu.VMEM((LMAX * KB, 1, LANES), jnp.int32),
                pltpu.SMEM((2 * shards, 1, LANES), jnp.int32),
                pltpu.SMEM((LMAX * KB, 1, LANES), jnp.int32),
                pltpu.SemaphoreType.DMA((4,)),
                pltpu.SemaphoreType.DMA((LMAX,)),
                pltpu.SemaphoreType.DMA,
                pltpu.SemaphoreType.DMA((shards,)),
                pltpu.SemaphoreType.DMA,
                pltpu.SemaphoreType.DMA((shards,)),
                pltpu.SemaphoreType.DMA,
                pltpu.SemaphoreType.DMA,
                pltpu.SemaphoreType.REGULAR,
                pltpu.SemaphoreType.DMA((STAGES,)),
                pltpu.SemaphoreType.DMA,
                pltpu.SemaphoreType.DMA((STAGES, shards)),
            ],
            compiler_params=pltpu.CompilerParams(
                collective_id=0, has_side_effects=True, vmem_limit_bytes=60 * 1024 * 1024
            ),
        )(depth, pending, arriving, coefficients, offsets, lookup)

    placed = (
        P("segment", None, "neuron"),
        P(None, None, "neuron"),
        P("segment", None, None, None, "neuron"),
        P("segment", None, "neuron"),
        P("segment", None, None, "neuron"),
        P("segment"),
    )
    return jax.shard_map(
        per_device,
        mesh=mesh,
        in_specs=placed,
        out_specs=P("segment", None, "neuron"),
        check_vma=False,
    )
```

time: 51.4 us -> 43.3 us (0.84)
  local copies, waits for them, and re-layouts: 5.93 us -> 1.47 us
  Pallas kernels: 44.5 us -> 40.9 us
    unnamed x11 -> x1, local copies, waits for them, and re-layouts: 5.93 us -> 1.47 us
    pallas_call x1, Pallas kernels: 44.5 us -> 40.9 us  [per_device(): pl.pallas_call(functools.partial(kernel, segments, shards), out_shape=jax...]
where the time goes in v2:
time: 43.3 us; the launch traced here: 43.1 us
  Pallas kernels  40.9 us (94%)
  local copies, waits for them, and re-layouts  1.47 us (3%)
  between operations  0.66 us (2%)
    pallas_call x1, Pallas kernels, per_device(): pl.pallas_call(functools.partial(kernel, segments, shards), out_shape=jax...  40.9 us
    unnamed x1, local copies, waits for them, and re-layouts  1.47 us

profile of v2, /device:TPU:1, one launch (start us, length us, event | category | flops | bytes accessed | tf_op | source)
XLA Modules:
  0.0 43.1 jit_solution(9710461054502111223)
XLA Ops:
  0.7 40.9 %shard_map.64 = bf16[1,8,4096]{2,1,0:T(8,128)(2,1)} custom-call(s32[1]{0:T(128)S(6)} %copy.8.depth_ref, bf16[1,8,4096]{2,1,0:T(8,128)(2,1)} %pending_ref.1, bf16[1,8,4096]{2,1,0:T(8,128)(2,1)} %arriving_ref.1, bf16[1,2,4,64,4096]{4,3,2,1,0:T(8,128)(2,1)} %weight_ref.1, f32[1,2,4096]{2,1,0:T(2,128)} %offset_ref.1, s32[1,2,4,64]{3,2,1,0:T(4,128)} %idx_ref.1), custom_call_target="tpu_custom_call" | custom-call | tf_op jit(solution)/shard_map/pallas_call | solution.py:384
  41.6 1.5 %copy.9 = bf16[1,8,4096]{2,1,0:T(8,128)(2,1)} copy(bf16[1,8,4096]{2,1,0:T(8,128)(2,1)} %shard_map.64) | data formatting | bytes 131072

commit v3 on v2

--- a/solution.py
+++ b/solution.py
@@ -280,15 +280,20 @@
             gather_for(own, t % LMAX, p, send.at[t], p)
             give(t, seg, p, send.at[t], send_sem.at[t], i == shards - 1)
 
-    def send_across(t):
+    def take_next_lists():
+        later = pl.ds(shards, shards)
+
         @pl.when(jnp.logical_not(last))
         def _():
-            later = pl.ds(shards, shards)
             pltpu.make_async_copy(wants, arrived.at[later], next_sem).wait()
             every = pltpu.make_async_copy(arrived.at[later], lists.at[later], slot_sem)
             every.start()
             pl.semaphore_wait(next_here, 1)
             every.wait()
+
+    def send_across(t):
+        @pl.when(jnp.logical_not(last))
+        def _():
             for p in far:
                 gather_for(own, 0, shards + p, send.at[t], p)
                 give(t, after, p, send.at[t], send_sem.at[t], False)
@@ -341,6 +346,7 @@
     send_first()
     apply(0)
     send_within(1)
+    take_next_lists()
     apply(1)
     send_across(2)
     apply(2)

time: 43.3 us -> 42.6 us (0.984)
  Pallas kernels: 40.9 us -> 40.2 us
    pallas_call x1, Pallas kernels: 40.9 us -> 40.2 us  [per_device(): pl.pallas_call(functools.partial(kernel, segments, shards), out_shape=jax...]
where the time goes in v3:
time: 42.6 us; the launch traced here: 42.4 us
  Pallas kernels  40.2 us (94%)
  local copies, waits for them, and re-layouts  1.47 us (3%)
  between operations  0.66 us (2%)
    pallas_call x1, Pallas kernels, per_device(): pl.pallas_call(functools.partial(kernel, segments, shards), out_shape=jax...  40.2 us
    unnamed x1, local copies, waits for them, and re-layouts  1.47 us

profile of v3, /device:TPU:1, one launch (start us, length us, event | category | flops | bytes accessed | tf_op | source)
XLA Modules:
  0.0 42.4 jit_solution(2926590522108149835)
XLA Ops:
  0.7 40.2 %shard_map.64 = bf16[1,8,4096]{2,1,0:T(8,128)(2,1)} custom-call(s32[1]{0:T(128)S(6)} %copy.8.depth_ref, bf16[1,8,4096]{2,1,0:T(8,128)(2,1)} %pending_ref.1, bf16[1,8,4096]{2,1,0:T(8,128)(2,1)} %arriving_ref.1, bf16[1,2,4,64,4096]{4,3,2,1,0:T(8,128)(2,1)} %weight_ref.1, f32[1,2,4096]{2,1,0:T(2,128)} %offset_ref.1, s32[1,2,4,64]{3,2,1,0:T(4,128)} %idx_ref.1), custom_call_target="tpu_custom_call" | custom-call | tf_op jit(solution)/shard_map/pallas_call | solution.py:390
  40.9 1.5 %copy.9 = bf16[1,8,4096]{2,1,0:T(8,128)(2,1)} copy(bf16[1,8,4096]{2,1,0:T(8,128)(2,1)} %shard_map.64) | data formatting | bytes 131072

commit v4 on v3

--- a/solution.py
+++ b/solution.py
@@ -11,7 +11,6 @@
 KB = 4
 LMAX = 2
 STAGES = 4
-NEAR = 11
 LANES = 128
 SIDE = 4
 MESH = pl.DeviceIdType.MESH
@@ -246,11 +245,10 @@
             gather_for(own, 0, near[i], send.at[0], near[i])
             give(0, seg, near[i], send.at[0], send_sem.at[0], i == 0)
 
-        for group in (range(NEAR), range(NEAR, shards)):
-            for i in group:
-                list_take(near[i])
-            for i in reversed(group):
-                one(i)
+        for i in range(shards):
+            list_take(near[i])
+        for i in reversed(range(shards)):
+            one(i)
 
         @pl.when(jnp.logical_not(first))
         def _():
@@ -306,15 +304,14 @@
             ).wait()
         half = shards * per_source // 2
         deep = per_source // 2
-        for group in (near[:NEAR], near[NEAR:]):
-            for v in group:
-                pltpu.make_async_copy(
-                    send.at[t, block_rows(v)], recv.at[t, block_rows(v)], recv_sem.at[t, v]
-                ).wait()
-            for v in group:
-                got = recv[t, block_rows(v), :].astype(jnp.float32).reshape(deep, 8, LANES)
-                table[pl.ds(v * deep, deep)] = got
-                table[pl.ds(half + v * deep, deep)] = pltpu.roll(got, BLK, 2)
+        for v in near:
+            pltpu.make_async_copy(
+                send.at[t, block_rows(v)], recv.at[t, block_rows(v)], recv_sem.at[t, v]
+            ).wait()
+        for v in near:
+            got = recv[t, block_rows(v), :].astype(jnp.float32).reshape(deep, 8, LANES)
+            table[pl.ds(v * deep, deep)] = got
+            table[pl.ds(half + v * deep, deep)] = pltpu.roll(got, BLK, 2)
         side = jnp.concatenate([low] * 4, axis=0)
         fresh = []
         for c in range(column_tiles // 2):

time: 42.6 us -> 42.2 us (level)
  no operation moved by 1% of the time
where the time goes in v4:
time: 42.2 us; the launch traced here: 42 us
  Pallas kernels  39.9 us (95%)
  local copies, waits for them, and re-layouts  1.47 us (3%)
  between operations  0.66 us (2%)
    pallas_call x1, Pallas kernels, per_device(): pl.pallas_call(functools.partial(kernel, segments, shards), out_shape=jax...  39.9 us
    unnamed x1, local copies, waits for them, and re-layouts  1.47 us

profile of v4, /device:TPU:1, one launch (start us, length us, event | category | flops | bytes accessed | tf_op | source)
XLA Modules:
  0.0 42.0 jit_solution(12482404163868391985)
XLA Ops:
  0.7 39.9 %shard_map.64 = bf16[1,8,4096]{2,1,0:T(8,128)(2,1)} custom-call(s32[1]{0:T(128)S(6)} %copy.8.depth_ref, bf16[1,8,4096]{2,1,0:T(8,128)(2,1)} %pending_ref.1, bf16[1,8,4096]{2,1,0:T(8,128)(2,1)} %arriving_ref.1, bf16[1,2,4,64,4096]{4,3,2,1,0:T(8,128)(2,1)} %weight_ref.1, f32[1,2,4096]{2,1,0:T(2,128)} %offset_ref.1, s32[1,2,4,64]{3,2,1,0:T(4,128)} %idx_ref.1), custom_call_target="tpu_custom_call" | custom-call | tf_op jit(solution)/shard_map/pallas_call | solution.py:387
  40.5 1.5 %copy.9 = bf16[1,8,4096]{2,1,0:T(8,128)(2,1)} copy(bf16[1,8,4096]{2,1,0:T(8,128)(2,1)} %shard_map.64) | data formatting | bytes 131072
